TPU v7x, 128 devices: a whole 4x4x4 slice. The times are simulated.
128 devices in a mesh: panel: 2 (over y_lo), lon: 16 (over y_hi, z, core), colat: 4 (over x).
Axes of the slice: x: 4, y: 4 (y_hi: 2, y_lo: 2; y = y_hi * 2 + y_lo), z: 4, core: 2. Of those that a mesh axis runs over, the one named last changes fastest.
Arguments:
- state: float32 [2, 8, 4, 768, 512], P('panel', None, None, 'lon', 'colat'), may hold values from -2 to 2
- send_base: int32 [2, 64, 240], P('panel', ('lon', 'colat')), may hold values from 0 to 6014, as said below
- send_frac: float32 [2, 64, 2, 240], P('panel', ('lon', 'colat')), may hold values from 0 to 1
- recv_slots: int32 [2, 64, 1056], P('panel', ('lon', 'colat')), may hold values from -1 to 15359, as said below
Outputs:
- new_state: float32 [2, 8, 4, 768, 512], P('panel', None, None, 'lon', 'colat')
Inputs may be any that keep to these rules, and one draw needn't show every extreme that they name: `send_base`: A flat offset on the sender tile's block whose four stencil cells base, base + 1, base + 128, base + 129 lie on that block, in every slot. `recv_slots`: -1 exactly on the sides of a tile that lie inside its panel; every border cell outside the panel names a slot s * 240 + c of sender tile s of the other panel, each slot at most once. Which slots are used is drawn; some sender tile has all 240 of its slots used.
All inputs are finite; a program needn't handle non-finite values.
Results may differ from a plain program's by a relative error of at most 0.0003.
Values sent between devices are 32-bit elements; how exact they have to be, the bound alone decides.
A program may use at most 64 MiB of HBM per device.

v0:
```python
import math

import jax
import jax.numpy as jnp
from jax import lax
from jax.experimental import pallas as pl
from jax.experimental.pallas import tpu as pltpu
from jax.sharding import PartitionSpec as P

MESH = pl.DeviceIdType.MESH
F32, BF16, I32 = jnp.float32, jnp.bfloat16, jnp.int32

QUANTITIES = 8
SHELLS = 4
FLAT = QUANTITIES * SHELLS
LON = 48
COL = 128
HALO = 3
OUT = 240
SIDE = HALO * LON
SLOTS = 256
GROUP = 8
GROUPS = 8
AROUND = (1, 3, 2)
SPARE = SIDE - COL
PART = FLAT // 2
TARGETS = 2 * GROUPS
TILES = 12
RING = 4
FOLD = PART // 8
STRIDE = LON + 16
TIME_STEP = 0.25
SPREAD = 0.1 / 3.0
S, MR, MT, MP, BR, BT, BP, WARM = range(QUANTITIES)


def dot(left, right):
    return jnp.dot(left, right, preferred_element_type=F32)


def split(value):
    high = value.astype(BF16)
    return high, (value - high.astype(F32)).astype(BF16)


def iota(shape, dim):
    return lax.broadcasted_iota(I32, shape, dim)


def cross_radial(m, b):
    return m[1] * b[2] - m[2] * b[1]


def cross_polar(m, b):
    return m[2] * b[0] - m[0] * b[2]


def cross_azimuthal(m, b):
    return m[0] * b[1] - m[1] * b[0]


def edge_rates(own, d, lap, emf_first, emf_second, along_lanes):
    grow, thin = jnp.exp(own[WARM]), jnp.exp(-own[S])
    b = own[BR:WARM]
    if along_lanes:
        vel, out = own[MT], MT
        lorentz = (d[BR] * b[1], -d[BR] * b[0] - d[BP] * b[2], d[BP] * b[1])
        turn = (emf_first, None, -emf_second)
    else:
        vel, out = own[MP], MP
        lorentz = (d[BR] * b[2], d[BT] * b[2], -d[BT] * b[1] - d[BR] * b[0])
        turn = (-emf_first, emf_second, None)
    result = [-vel * d[S] - d[out]]
    for i in range(3):
        rate = -vel * d[MR + i] + thin * lorentz[i] + SPREAD * lap[MR + i]
        if MR + i == out:
            rate = rate - grow * (d[S] + d[WARM])
        result.append(rate)
    for i in range(3):
        rate = SPREAD * lap[BR + i]
        result.append(rate if turn[i] is None else rate + turn[i])
    result.append(-vel * d[WARM] - (2.0 / 3.0) * d[out] + SPREAD * lap[WARM])
    return result


def shell_first(x):
    a, b = 8.0 * (x[3] - x[0]), 45.0
    return (
        b * (x[1] - x[0]) - 9.0 * (x[2] - x[0]) + (x[3] - x[0]),
        b * (x[2] - x[0]) - a,
        b * (x[3] - x[1]) - a,
        b * (x[3] - x[2]) - 9.0 * (x[3] - x[1]) + (x[3] - x[0]),
    )


def shell_second(x):
    return (
        2.0 * x[3] - 27.0 * x[2] + 270.0 * x[1] - 245.0 * x[0],
        245.0 * x[0] - 490.0 * x[1] + 270.0 * x[2] - 25.0 * x[3],
        245.0 * x[3] - 490.0 * x[2] + 270.0 * x[1] - 25.0 * x[0],
        2.0 * x[0] - 27.0 * x[1] + 270.0 * x[2] - 245.0 * x[3],
    )


def turn_edges(col_add, turned):
    for side in range(2):
        for j in range(HALO):
            for half in range(2):
                turned[half, pl.ds((1 - side) * HALO + j, FLAT // 2, stride=8), :] = col_add[
                    side, j, half * (FLAT // 2) : (half + 1) * (FLAT // 2), :
                ]


def field_edge(edge, g):
    lane = iota((LON, COL), 1)
    border = jnp.logical_or(lane < HALO, lane >= COL - HALO)
    return jnp.where(border, pltpu.roll(edge, COL - 8 * g - HALO, 1), 0.0)


def closing(value_ref, row_add, col_add, out_hbm, turned, ready, sem):
    turn_edges(col_add, turned)
    copies = []
    for half in range(2):
        edge = jnp.transpose(turned[half])[0:LON, :]
        for chunk in range(2):
            first = half * (FLAT // 2) + 8 * chunk
            for q in range(8):
                at = (first + q) * LON
                ready[at : at + LON, :] = value_ref[at : at + LON, :] + field_edge(edge, 8 * chunk + q)
            for side in range(2):
                for j in range(HALO):
                    rows = pl.ds(first * LON + (j if side == 0 else LON - HALO + j), 8, stride=LON)
                    ready[rows, :] = ready[rows, :] + row_add[side, j, first : first + 8, :]
            rows = pl.ds(first * LON, 8 * LON)
            copy = pltpu.make_async_copy(ready.at[rows, :], out_hbm.at[rows, :], sem.at[2 * half + chunk])
            copy.start()
            copies.append(copy)
    for copy in copies:
        copy.wait()


def kernel(
    x_hbm, base_hbm, frac_hbm, slots_hbm, out_ref, row_add, col_add,
    deep, base_ref, frac_ref, slots_ref, emf, lanes, mix, cols_mix, rows_mix, rows_split, band, onehot, owner, turned,
    blocks, table, idx_out, idx_in, rest_rows, picked, picked_rows, got_cols, got_rows, row_out, row_in, col_own, col_out, col_in,
    row_halo, col_halo,
    in_sem, idx_send, idx_recv, a_send, a_recv, s_send, b_send, b_recv, l_send, l_recv, r_send, r_recv, c_send, c_recv,
):
    panel, lon, col = lax.axis_index("panel"), lax.axis_index("lon"), lax.axis_index("colat")
    n_lon, n_col = lax.axis_size("lon"), lax.axis_size("colat")
    core, mine = lon & 1, lon >> 1
    member = core * n_col + col
    other = 1 - panel
    lon_up, lon_down = lax.rem(lon + 1, n_lon), lax.rem(lon + n_lon - 1, n_lon)
    col_up, col_down = lax.rem(col + 1, n_col), lax.rem(col + n_col - 1, n_col)
    outer = lax.rem(lon + 2 * core - 1 + n_lon, n_lon)
    sends_rows = (lon < n_lon - 1, lon > 0)
    sends_cols = (col < n_col - 1, col > 0)
    col_edge = jnp.logical_or(col == 0, col == n_col - 1)

    sibling = (panel, lon + 1 - 2 * core, col)
    origin = core * GROUPS + mine

    def row_device(step, half):
        return (panel, 2 * mine + half, (col + step) & (n_col - 1))

    def target_device(target):
        return (other, 2 * (target & (GROUPS - 1)) + (target >> 3), col)

    def remote(src, dst, send, recv, device):
        return pltpu.make_async_remote_copy(
            src_ref=src, dst_ref=dst, send_sem=send, recv_sem=recv, device_id=device, device_id_type=MESH
        )

    frame = deep.reshape(2, FLAT * STRIDE, COL)
    copies = [
        pltpu.make_async_copy(src, dst, in_sem.at[i])
        for i, (src, dst) in enumerate(
            (
                (frac_hbm, frac_ref),
                (base_hbm, base_ref),
                (slots_hbm, slots_ref),
                (x_hbm, deep.at[0, :, pl.ds(8, LON), :]),
            )
        )
    ]
    for copy in copies:
        copy.start()

    barrier = pltpu.get_barrier_semaphore()
    for step in AROUND:
        for half in range(2):
            pl.semaphore_signal(barrier, inc=1, device_id=row_device(step, half), device_id_type=MESH)
    pl.semaphore_signal(barrier, inc=1, device_id=sibling, device_id_type=MESH)
    for target in range(TARGETS):
        pl.semaphore_signal(barrier, inc=1, device_id=target_device(target), device_id_type=MESH)
    pl.semaphore_signal(barrier, inc=1, device_id=(panel, outer, col), device_id_type=MESH)

    copies[0].wait()
    copies[1].wait()
    base = jnp.concatenate([base_ref[...], jnp.zeros((1, SLOTS - OUT), I32)], axis=1)
    base_row, base_col = lax.div(base, COL), lax.rem(base, COL)
    share = jnp.concatenate([frac_ref[...], jnp.zeros((2, SLOTS - OUT), F32)], axis=1)
    along, across = share[0:1, :], share[1:2, :]
    cells = iota((COL, SLOTS), 0)
    weight = jnp.where(cells == base_col, 1.0 - across, 0.0) + jnp.where(cells == base_col + 1, across, 0.0)
    weight_high, weight_low = split(weight)
    cols_mix[...] = weight
    mix[0:COL, :] = weight_high
    mix[COL : 2 * COL, :] = weight_high
    mix[2 * COL : 3 * COL, :] = weight_low
    cells = iota((LON, SLOTS), 0)
    weight = jnp.where(cells == base_row, 1.0 - along, 0.0) + jnp.where(cells == base_row + 1, along, 0.0)
    rows_mix[...] = weight
    place = (col * COL + iota((1, COL), 1)).astype(F32)
    scale = 1.0 / jnp.sin(math.pi / 4.0 + (place + 0.5) * (math.pi / 2.0 / (COL * n_col)))

    def message_tables():
        copies[2].wait()
        spot = iota((1, SLOTS), 1)
        sides = jnp.where(spot < SIDE, jnp.maximum(slots_ref[:, 0:SLOTS], slots_ref[:, SIDE : SIDE + SLOTS]) + 1, 0)
        digits = jnp.concatenate([lax.div(sides, COL), lax.rem(sides, COL), jnp.zeros((6, SLOTS), I32)], axis=0)
        source, target = iota((SLOTS, SLOTS), 0), iota((SLOTS, SLOTS), 1)
        layer = jnp.where(target >= LON, 1, 0) + jnp.where(target >= 2 * LON, 1, 0)
        order = jnp.logical_and(target < SIDE, source == HALO * (target - LON * layer) + layer)
        digits = dot(digits.astype(F32).astype(BF16), jnp.where(order, 1.0, 0.0).astype(BF16)).astype(I32)
        sides = digits[0:1, :] * COL + digits[1:2, :] - 1
        idx_out[0:1, :] = sides[:, 0:COL]
        idx_out[1:2, :] = sides[:, COL : 2 * COL]
        for h in range(HALO):
            at = 2 * SIDE + h * COL
            idx_out[2 + h : 3 + h, :] = jnp.maximum(
                slots_ref[:, at : at + COL], slots_ref[:, at + HALO * COL : at + HALO * COL + COL]
            )
        idx_out[5:8, :] = jnp.full((3, COL), -1, I32)

    def other_tables():
        zero_rows = jnp.zeros((8, COL), F32)
        for f in range(FLAT):
            for part in range(2):
                frame[part, f * STRIDE : f * STRIDE + 8, :] = zero_rows
                frame[part, f * STRIDE + 8 + LON : (f + 1) * STRIDE, :] = zero_rows
        for f in range(3 * SHELLS):
            emf[f * STRIDE : f * STRIDE + 8, :] = zero_rows
            emf[f * STRIDE + 8 + LON : (f + 1) * STRIDE, :] = zero_rows

        for half in range(2):
            turned[half, :, :] = jnp.zeros((COL, COL), F32)

        apart = iota((COL, COL), 0) - iota((COL, COL), 1)
        reach = jnp.abs(apart)
        first = jnp.where(reach == 1, 45.0, jnp.where(reach == 2, -9.0, jnp.where(reach == 3, 1.0, 0.0)))
        first = jnp.where(apart < 0, -first, first).astype(BF16)
        second = jnp.where(
            reach == 0, -490.0, jnp.where(reach == 1, 270.0, jnp.where(reach == 2, -27.0, jnp.where(reach == 3, 2.0, 0.0)))
        ).astype(BF16)
        for part in range(2):
            band[part * COL : (part + 1) * COL, 0:COL] = first
            band[part * COL : (part + 1) * COL, COL : 2 * COL] = second
        weight_high, weight_low = split(jnp.concatenate([rows_mix[...], jnp.zeros((COL - LON, SLOTS), F32)], axis=0))
        rows_split[0:COL, :] = weight_high
        rows_split[COL : 2 * COL, :] = weight_high
        rows_split[2 * COL : 3 * COL, :] = weight_low

    def load_split(part, pair):
        block = jnp.concatenate(
            [frame[part, pl.ds(pl.multiple_of((8 * pair + q) * STRIDE + 8, 8), LON), :] for q in range(8)], axis=0
        )
        return split(block)

    def interpolate(part, half):
        for pair in range(PART // 8):
            high, low = load_split(part, 2 * half + pair)
            value = dot(jnp.concatenate([high, low, high], axis=1), mix[...])
            value = jnp.sum(value.reshape(8, LON, SLOTS) * rows_mix[...][None], axis=1)
            blocks[part, half, 8 * pair : 8 * pair + 8, :] = value

    def send(part, half):
        for step in AROUND:
            a_copy(part, step, half).start()

        @pl.when(core != half)
        def _():
            s_copy(part, half).start()

        @pl.when(core == half)
        def _():
            table[part, member] = blocks[part, half]

    def lane_pass(part):
        def body(pair, carry):
            high, low = load_split(part, pair)
            both = jnp.concatenate([high, low], axis=1)
            lanes[pl.ds(pl.multiple_of(8 * LON * pair, 8), 8 * LON), :] = dot(both, band[...])
            return carry

        lax.fori_loop(0, FLAT // 8, body, 0)

    def cols_of(part):
        lane = iota((LON, COL), 1)
        for half in range(2):
            edge = jnp.zeros((LON, COL), F32)
            for g in range(FLAT // 2):
                at = (half * (FLAT // 2) + g) * STRIDE + 8
                moved = pltpu.roll(frame[part, at : at + LON, :], 8 * g + HALO, 1)
                edge = jnp.where(jnp.logical_and(lane >= 8 * g, lane < 8 * g + 2 * HALO), moved, edge)
            turned[half, :, 0:LON] = jnp.transpose(edge)
        for side in range(2):
            for j in range(HALO):
                first = (1 - side) * HALO + j
                for half in range(2):
                    col_own[part, side, j, half * (FLAT // 2) : (half + 1) * (FLAT // 2), :] = turned[
                        half, pl.ds(first, FLAT // 2, stride=8), :
                    ]
            col_out[part, side, 0] = jnp.where(
                iota((FLAT, COL), 1) < COL // 2, col_own[part, side, 0], pltpu.roll(col_own[part, side, 1], COL // 2, 1)
            )
            col_out[part, side, 1] = col_own[part, side, 2]

    def emf_pass(part):
        for r in range(SHELLS):
            def field(q):
                at = (q * SHELLS + r) * STRIDE + 8
                return frame[part, at : at + LON, :]

            m, b = [field(MR + i) for i in range(3)], [field(BR + i) for i in range(3)]
            for i, form in enumerate((cross_radial, cross_polar, cross_azimuthal)):
                at = (i * SHELLS + r) * STRIDE + 8
                emf[at : at + LON, :] = form(m, b)
        for i, at in ((0, FLAT), (2, FLAT + SHELLS)):
            block = jnp.concatenate(
                [emf[(i * SHELLS + r) * STRIDE + 8 : (i * SHELLS + r) * STRIDE + 8 + LON, :] for r in range(SHELLS)],
                axis=0,
            )
            high, low = split(block)
            lanes[at * LON : (at + SHELLS) * LON, 0:COL] = dot(
                jnp.concatenate([high, low], axis=1), band[:, 0:COL]
            )

    def main_pass(part, start, stop):
        def body(block, carry):
            here = pl.multiple_of(8 * block, 8)

            def near(f, apart):
                return frame[part, pl.ds(f * STRIDE + 8 + here + apart, 8), :]

            def near_emf(f, apart):
                return emf[pl.ds(f * STRIDE + 8 + here + apart, 8), :]

            def lane_first(f):
                return lanes[pl.ds(f * LON + here, 8), 0:COL]

            def lane_second(f):
                return lanes[pl.ds(f * LON + here, 8), COL : 2 * COL]

            def row_first(at):
                return 45.0 * (at[1] - at[-1]) - 9.0 * (at[2] - at[-2]) + (at[3] - at[-3])

            def row_second(at, centre):
                return (
                    270.0 * (at[1] + at[-1]) - 27.0 * (at[2] + at[-2]) + 2.0 * (at[3] + at[-3]) - 490.0 * centre
                )

            centre = [[near(q * SHELLS + r, 0) for r in range(SHELLS)] for q in range(QUANTITIES)]
            radial = [shell_first(x) for x in centre]
            radial_second = [None if q == S else shell_second(centre[q]) for q in range(QUANTITIES)]
            emf_centre = [[near_emf(i * SHELLS + r, 0) for r in range(SHELLS)] for i in range(3)]
            emf_radial = [None, shell_first(emf_centre[1]), shell_first(emf_centre[2])]
            for r in range(SHELLS):
                own = [centre[q][r] for q in range(QUANTITIES)]
                g, lap = [], []
                for q in range(QUANTITIES):
                    f = q * SHELLS + r
                    at = {d: near(f, d) for d in (-3, -2, -1, 1, 2, 3)}
                    g.append((radial[q][r], lane_first(f), scale * row_first(at)))
                    if q == S:
                        lap.append(None)
                    else:
                        lap.append(
                            radial_second[q][r] + lane_second(f) + (scale * scale) * row_second(at, own[q])
                        )
                m, b = own[MR:BR], own[BR:WARM]

                def advect(q):
                    return m[0] * g[q][0] + m[1] * g[q][1] + m[2] * g[q][2]

                div = g[MR][0] + g[MT][1] + g[MP][2]
                current = (g[BP][1] - g[BT][2], g[BR][2] - g[BP][0], g[BT][0] - g[BR][1])
                lorentz = (
                    current[1] * b[2] - current[2] * b[1],
                    current[2] * b[0] - current[0] * b[2],
                    current[0] * b[1] - current[1] * b[0],
                )
                grow, thin = jnp.exp(own[WARM]), jnp.exp(-own[S])
                emf_rows = {}
                for i in (0, 1):
                    f = i * SHELLS + r
                    emf_rows[i] = scale * row_first({d: near_emf(f, d) for d in (-3, -2, -1, 1, 2, 3)})
                turn = (
                    lane_first(FLAT + SHELLS + r) - emf_rows[1],
                    emf_rows[0] - emf_radial[2][r],
                    emf_radial[1][r] - lane_first(FLAT + r),
                )
                result = [-advect(S) - div]
                for i in range(3):
                    result.append(
                        -advect(MR + i) - grow * (g[S][i] + g[WARM][i]) + thin * lorentz[i] + SPREAD * lap[MR + i]
                    )
                for i in range(3):
                    result.append(turn[i] + SPREAD * lap[BR + i])
                result.append(-advect(WARM) - (2.0 / 3.0) * div + SPREAD * lap[WARM])
                for q in range(QUANTITIES):
                    f = q * SHELLS + r
                    value = own[q] + (TIME_STEP / 60.0) * result[q]
                    if part == 0:
                        frame[1, pl.ds(f * STRIDE + 8 + here, 8), :] = value
                    else:
                        start = frame[0, pl.ds(f * STRIDE + 8 + here, 8), :]
                        out_ref[pl.ds(f * LON + here, 8), :] = 0.5 * (start + value)
            return carry

        lax.fori_loop(start, stop, body, 0)

    def rows_of(part):
        for h in range(HALO):
            row_out[part, 0, h] = frame[part, pl.ds(8 + h, FLAT, stride=STRIDE), :]
            row_out[part, 1, h] = frame[part, pl.ds(8 + LON - HALO + h, FLAT, stride=STRIDE), :]

    def prepare_picks():
        for tile in range(2 * TILES):
            if tile < TARGETS:
                slot = idx_in[tile, 0:1, :]
            elif tile < TARGETS + 2:
                first = (tile - TARGETS) * GROUPS
                slot = idx_in[first, 1:2, :]
                for q in range(1, GROUPS):
                    slot = jnp.maximum(slot, pltpu.roll(idx_in[first + q], SPARE * q, 1)[1:2, :])
            else:
                side, h = divmod(tile - TARGETS - 2, HALO)
                slot = idx_in[side * (TARGETS - 1), 2 + h : 3 + h, :]
            slot = slot - mine * (GROUP * OUT)
            who = jnp.zeros_like(slot)
            for q in range(1, GROUP):
                who = who + jnp.where(slot >= q * OUT, 1, 0)
            cell = slot - who * OUT
            who = jnp.where(jnp.logical_and(slot >= 0, slot < GROUP * OUT), who, -1)
            at = (tile % 2) * COL
            owner[tile // 2, :, at : at + COL] = jnp.broadcast_to(who, (8, COL))
            hot = jnp.where(iota((SLOTS, COL), 0) == cell, 1.0, 0.0).astype(BF16)
            onehot[tile // 2, :, at : at + COL] = hot

    def table_split(part):
        high, low = split(table[part].reshape(GROUP * PART, SLOTS))
        return jnp.concatenate([high, low], axis=0)

    def product(both, tile):
        return dot(both, onehot[tile])

    def chosen(value, tile):
        value = value[0 : GROUP * PART] + value[GROUP * PART :]
        who = jnp.broadcast_to(owner[tile, 0:1, :], (PART, SLOTS))
        total = jnp.zeros((PART, SLOTS), F32)
        for q in range(GROUP):
            total = jnp.where(who == q, value[q * PART : (q + 1) * PART, :], total)
        return total[:, 0:COL], total[:, COL : 2 * COL]

    def fold(rests):
        turn = (lax.div(iota((8, COL), 1), SPARE) - iota((8, COL), 0)) & 7
        for half, rest in enumerate(rests):
            for s in range(FOLD):
                total = jnp.zeros((8, COL), F32)
                for d in range(8):
                    moved = rest[8 * s : 8 * s + 8, :]
                    if d:
                        moved = pltpu.roll(pltpu.roll(moved, SPARE * d, 1), 8 - d, 0)
                    total = jnp.where(turn == d, moved, total)
                rest_rows[half, s] = total

    def pick_all(part, both):
        sides = [(step + mine) & (TARGETS // 2 - 1) for step in range(TARGETS // 2)]
        extra = list(range(TARGETS // 2 + 1, TILES))
        ends, value = [], product(both, extra[0])
        for tile, after in zip(extra, extra[1:] + [None]):
            now = value
            if after is not None:
                value = product(both, after)
            ends += chosen(now, tile)
        for side in range(2):
            for h in range(HALO):
                picked_rows[part, side, h] = ends[side * HALO + h]
        for side in range(2):
            l_copy(part, side).start()

        @pl.when(col_edge)
        def _():
            now, value = product(both, TARGETS // 2), product(both, sides[0])
            fold(chosen(now, TARGETS // 2))
            for step, tile in enumerate(sides):
                now = value
                if step + 1 < len(sides):
                    value = product(both, sides[step + 1])
                for i, end in enumerate(chosen(now, tile)):
                    target = 2 * tile + i
                    picked[part, target, 0:PART, :] = end
                    for s in range(FOLD):
                        picked[part, target, PART + s : PART + s + 1, :] = rest_rows[
                            tile >> 2, s, pl.ds(target & (GROUPS - 1), 1), :
                        ]
                for i in range(2):
                    b_copy(part, 2 * tile + i).start()

    def corrections(part, side, along_lanes):
        halo_ref, own_ref, add_ref = (col_halo, col_own, col_add) if along_lanes else (row_halo, row_out, row_add)

        def scaled(value, power):
            for _ in range(0 if along_lanes else power):
                value = scale * value
            return value

        halo = [[halo_ref[side, h, q * SHELLS : (q + 1) * SHELLS, :] for q in range(QUANTITIES)] for h in range(HALO)]
        form = cross_azimuthal if along_lanes else cross_polar
        halo_emf = [(cross_radial(x[MR:BR], x[BR:WARM]), form(x[MR:BR], x[BR:WARM])) for x in halo]
        sign = -1.0 if side == 0 else 1.0
        firsts, seconds = (45.0 * sign, -9.0 * sign, sign), (270.0, -27.0, 2.0)
        for j in range(HALO):
            own = [own_ref[part, side, j, q * SHELLS : (q + 1) * SHELLS, :] for q in range(QUANTITIES)]

            def total(weights, of):
                result = None
                for m in (1, 2, 3):
                    h = j + 3 - m if side == 0 else m - 3 + j
                    if 0 <= h < HALO:
                        term = weights[m - 1] * of(h)
                        result = term if result is None else result + term
                return result

            d = [scaled(total(firsts, lambda h, q=q: halo[h][q]), 1) for q in range(QUANTITIES)]
            lap = [
                None if q == S else scaled(total(seconds, lambda h, q=q: halo[h][q]), 2) for q in range(QUANTITIES)
            ]
            radial = scaled(total(firsts, lambda h: halo_emf[h][0]), 1)
            second = scaled(total(firsts, lambda h: halo_emf[h][1]), 1)
            result = edge_rates(own, d, lap, second, radial, along_lanes)
            for q in range(QUANTITIES):
                add_ref[side, j, q * SHELLS : (q + 1) * SHELLS, :] = (TIME_STEP / 60.0 / (1 + part)) * result[q]

    def contribute(side, along_lanes):
        add_ref = col_add if along_lanes else row_add
        value = jnp.concatenate([add_ref[side, j] for j in range(HALO)], axis=0)
        if along_lanes:
            value = jnp.where(iota((HALO * FLAT, COL), 1) < LON, value, 0.0)
        high, low = split(value)
        value = dot(jnp.concatenate([high, low, high], axis=1), rows_split[...] if along_lanes else mix[...])
        total = jnp.zeros((FLAT, SLOTS), F32)
        for j in range(HALO):
            if along_lanes:
                at = j if side == 0 else COL - HALO + j
                weight = cols_mix[at : at + 1, :]
            else:
                at = j if side == 0 else LON - HALO + j
                weight = rows_mix[at : at + 1, :]
            total = total + weight * value[j * FLAT : (j + 1) * FLAT, :]
        for half in range(2):
            blocks[1, half] = blocks[1, half] + total[half * PART : (half + 1) * PART, :]

    def apply_edges():
        for side in range(2):
            for j in range(HALO):
                rows = pl.ds(8 + (j if side == 0 else LON - HALO + j), FLAT, stride=STRIDE)
                frame[1, rows, :] = frame[1, rows, :] + row_add[side, j]
        turn_edges(col_add, turned)
        for half in range(2):
            edge = jnp.transpose(turned[half])[0:LON, :]
            for g in range(FLAT // 2):
                at = (half * (FLAT // 2) + g) * STRIDE + 8
                frame[1, at : at + LON, :] = frame[1, at : at + LON, :] + field_edge(edge, g)

    def a_copy(part, step, half):
        return remote(
            blocks.at[part, half], table.at[part, member], a_send.at[part, half, step], a_recv.at[part, member],
            row_device(step, half),
        )

    def s_copy(part, half):
        return remote(
            blocks.at[part, half], table.at[part, member], s_send.at[part], a_recv.at[part, member], sibling
        )

    def a_arrival(part, step):
        there = (member + step) & (GROUP - 1)
        return remote(blocks.at[part, 0], table.at[part, there], s_send.at[part], a_recv.at[part, there], sibling)

    def b_copy(part, target):
        return remote(
            picked.at[part, target], got_cols.at[part, origin], b_send.at[part, target], b_recv.at[part, origin],
            target_device(target),
        )

    def b_arrival(part, source):
        return remote(
            picked.at[part, 0], got_cols.at[part, source], b_send.at[part, 0], b_recv.at[part, source],
            (other, lon, col),
        )

    def l_copy(part, side):
        return remote(
            picked_rows.at[part, side], got_rows.at[part, origin], l_send.at[part, side], l_recv.at[part, origin],
            target_device(side * (TARGETS - 1)),
        )

    def l_arrival(part, source):
        return remote(
            picked_rows.at[part, 0], got_rows.at[part, source], l_send.at[part, 0], l_recv.at[part, source],
            (other, lon, col),
        )

    def row_copy(part, side):
        return remote(
            row_out.at[part, 1 - side], row_in.at[part, side], r_send.at[part, side], r_recv.at[part, side],
            (panel, lon_up if side == 0 else lon_down, col),
        )

    def col_copy(part, side):
        return remote(
            col_out.at[part, 1 - side], col_in.at[part, side], c_send.at[part, side], c_recv.at[part, side],
            (panel, lon, col_up if side == 0 else col_down),
        )

    def idx_copy(target):
        return remote(
            idx_out, idx_in.at[origin], idx_send.at[target], idx_recv.at[origin], target_device(target)
        )

    def idx_arrival(source):
        return remote(idx_out, idx_in.at[source], idx_send.at[0], idx_recv.at[source], (other, lon, col))

    def inner_sides(part):
        for side in range(2):
            @pl.when(lon != (0 if side == 0 else n_lon - 1))
            def _():
                row_copy(part, side).wait_recv()
                row_halo[side] = row_in[part, side]
                corrections(part, side, False)
                if part == 0:
                    contribute(side, False)

            @pl.when(col != (0 if side == 0 else n_col - 1))
            def _():
                col_copy(part, side).wait_recv()
                pair = col_in[part, side, 0]
                col_halo[side, 0] = pair
                col_halo[side, 1] = pltpu.roll(pair, COL // 2, 1)
                col_halo[side, 2] = col_in[part, side, 1]
                corrections(part, side, True)
                if part == 0:
                    contribute(side, True)

    def outer_sides(part):
        for side in range(2):

            @pl.when(col == (0 if side == 0 else n_col - 1))
            def _():
                for source in range(TARGETS):
                    b_arrival(part, source).wait_recv()
                for half in range(2):
                    total = got_cols[part, half * GROUPS]
                    for group in range(1, GROUPS):
                        total = total + got_cols[part, half * GROUPS + group]
                    main = total[0:PART]
                    rows = slice(half * PART, (half + 1) * PART)
                    col_halo[side, 0, rows, :] = main
                    col_halo[side, 1, rows, :] = pltpu.roll(main, COL - LON, 1)
                    main = pltpu.roll(main, COL - 2 * LON, 1)
                    row, lane = iota((8, COL), 0), iota((8, COL), 1)
                    for s in range(FOLD):
                        value = main[8 * s : 8 * s + 8, :]
                        rest = jnp.broadcast_to(total[PART + s : PART + s + 1], (8, COL))
                        for q in range(8):
                            moved = pltpu.roll(rest, (2 * COL - 2 * LON - SPARE * q) % COL, 1)
                            value = jnp.where(jnp.logical_and(row == q, lane >= COL - 2 * LON), moved, value)
                        at = half * PART + 8 * s
                        col_halo[side, 2, at : at + 8, :] = value
                corrections(part, side, True)
                if part == 0:
                    contribute(side, True)

            @pl.when(lon == (0 if side == 0 else n_lon - 1))
            def _():
                for source in range(TARGETS):
                    l_arrival(part, source).wait_recv()
                for half in range(2):
                    total = got_rows[part, half * GROUPS]
                    for group in range(1, GROUPS):
                        total = total + got_rows[part, half * GROUPS + group]
                    row_halo[side, :, half * PART : (half + 1) * PART, :] = total
                corrections(part, side, False)
                if part == 0:
                    contribute(side, False)

    for part in range(2):
        if part == 0:
            message_tables()
            pl.semaphore_wait(barrier, 2 * len(AROUND) + 2 + TARGETS)
            for target in range(TARGETS):
                idx_copy(target).start()
            copies[3].wait()
            interpolate(0, 0)
            send(0, 0)
            interpolate(0, 1)
            send(0, 1)
            other_tables()
        else:
            send(1, 0)
            send(1, 1)
            apply_edges()
        rows_of(part)
        for side in range(2):

            @pl.when(sends_rows[side])
            def _():
                row_copy(part, side).start()

        cols_of(part)
        for side in range(2):

            @pl.when(sends_cols[side])
            def _():
                col_copy(part, side).start()

        lane_pass(part)
        emf_pass(part)
        if part == 0:
            for source in range(TARGETS):
                idx_arrival(source).wait_recv()
            prepare_picks()
        for step in range(1, GROUP):
            a_arrival(part, step).wait_recv()
        both = table_split(part)
        pick_all(part, both)
        main_pass(part, 0, 6)
        if part == 0:
            interpolate(1, 0)
            interpolate(1, 1)
        inner_sides(part)
        outer_sides(part)

    for target in range(TARGETS):
        idx_copy(target).wait_send()
    for part in range(2):
        for half in range(2):
            for step in AROUND:
                a_copy(part, step, half).wait_send()
        s_copy(part, 0).wait_send()
        for side in range(2):
            l_copy(part, side).wait_send()

            @pl.when(sends_rows[side])
            def _():
                row_copy(part, side).wait_send()

            @pl.when(sends_cols[side])
            def _():
                col_copy(part, side).wait_send()


        @pl.when(col_edge)
        def _():
            for target in range(TARGETS):
                b_copy(part, target).wait_send()


def shards(state, send_base, send_frac, recv_slots):
    rows = FLAT * LON
    dma = pltpu.SemaphoreType.DMA
    vmem = pltpu.VMEM
    scratch = [
        vmem((2, FLAT, STRIDE, COL), F32),
        vmem((1, OUT), I32),
        vmem((2, OUT), F32),
        vmem((1, recv_slots.shape[-1]), I32),
        vmem((3 * SHELLS * STRIDE, COL), F32),
        vmem(((FLAT + 2 * SHELLS) * LON, 2 * COL), F32),
        vmem((3 * COL, SLOTS), BF16),
        vmem((COL, SLOTS), F32),
        vmem((LON, SLOTS), F32),
        vmem((3 * COL, SLOTS), BF16),
        vmem((2 * COL, 2 * COL), BF16),
        vmem((TILES, SLOTS, 2 * COL), BF16),
        vmem((TILES, 8, 2 * COL), I32),
        vmem((2, COL, COL), F32),
        vmem((2, 2, PART, SLOTS), F32),
        vmem((2, GROUP, PART, SLOTS), F32),
        vmem((8, COL), I32),
        vmem((TARGETS, 8, COL), I32),
        vmem((2, FOLD, 8, COL), F32),
        vmem((2, TARGETS, PART + FOLD, COL), F32),
        vmem((2, 2, HALO, PART, COL), F32),
        vmem((2, TARGETS, PART + FOLD, COL), F32),
        vmem((2, TARGETS, HALO, PART, COL), F32),
        vmem((2, 2, HALO, FLAT, COL), F32),
        vmem((2, 2, HALO, FLAT, COL), F32),
        vmem((2, 2, HALO, FLAT, COL), F32),
        vmem((2, 2, 2, FLAT, COL), F32),
        vmem((2, 2, 2, FLAT, COL), F32),
        vmem((2, HALO, FLAT, COL), F32),
        vmem((2, HALO, FLAT, COL), F32),
        dma((4,)),
        dma((TARGETS,)),
        dma((TARGETS,)),
        dma((2, 2, RING)),
        dma((2, GROUP)),
        dma((2,)),
        dma((2, TARGETS)),
        dma((2, TARGETS)),
        dma((2, 2)),
        dma((2, TARGETS)),
        dma((2, 2)),
        dma((2, 2)),
        dma((2, 2)),
        dma((2, 2)),
    ]
    edges = jax.ShapeDtypeStruct((2, HALO, FLAT, COL), F32)
    value, row_add, col_add = pl.pallas_call(
        kernel,
        out_shape=(jax.ShapeDtypeStruct((rows, COL), F32), edges, edges),
        in_specs=[pl.BlockSpec(memory_space=pltpu.HBM)] * 4,
        out_specs=[pl.BlockSpec(memory_space=pltpu.VMEM)] * 3,
        scratch_shapes=scratch,
        compiler_params=pltpu.CompilerParams(
            collective_id=0, has_side_effects=True, vmem_limit_bytes=40 * 1024 * 1024
        ),
    )(*(
        pltpu.with_memory_space_constraint(x, pltpu.HBM)
        for x in (state.reshape(FLAT, LON, COL), send_base[0], send_frac[0, 0], recv_slots[0])
    ))
    result = pl.pallas_call(
        closing,
        out_shape=jax.ShapeDtypeStruct((rows, COL), F32),
        in_specs=[pl.BlockSpec(memory_space=pltpu.VMEM)] * 3,
        out_specs=pl.BlockSpec(memory_space=pltpu.HBM),
        scratch_shapes=[vmem((2, COL, COL), F32), vmem((rows, COL), F32), dma((4,))],
        compiler_params=pltpu.CompilerParams(vmem_limit_bytes=16 * 1024 * 1024),
    )(value, row_add, col_add)
    return result.reshape(state.shape)


def solution(mesh):
    placed = (
        P("panel", None, None, "lon", "colat"),
        P("panel", ("lon", "colat"), None),
        P("panel", ("lon", "colat"), None, None),
        P("panel", ("lon", "colat"), None),
    )
    return jax.shard_map(
        shards,
        mesh=mesh,
        in_specs=placed,
        out_specs=P("panel", None, None, "lon", "colat"),
        check_vma=False,
    )
```

profile of v0, /device:TPU:1, one launch (start us, length us, event | category | flops | bytes accessed | tf_op | source)
XLA Modules:
  0.0 31.9 jit_solution(4159102454315321280)
XLA Ops:
  0.0 30.7 %shard_map.46 = (f32[1536,128]{1,0:T(8,128)S(1)}, f32[2,3,32,128]{3,2,1,0:T(8,128)S(1)}, f32[2,3,32,128]{3,2,1,0:T(8,128)S(1)}) custom-call(f32[32,48,128]{2,1,0:T(8,128)} %bitcast.5, s32[1,240]{1,0:T(1,128)} %bitcast.8, f32[2,240]{1,0:T(2,128)} %bitcast.7, s32[1,1056]{1,0:T(1,128)} %bitcast.6), custom_call_target="tpu_custom_call" | custom-call | tf_op jit(solution)/shard_map/pallas_call | solution.py:823
  30.7 1.2 %shard_map.47 = f32[1536,128]{1,0:T(8,128)} custom-call(f32[1536,128]{1,0:T(8,128)S(1)} %get-tuple-element.8.value_ref, f32[2,3,32,128]{3,2,1,0:T(8,128)S(1)} %get-tuple-element.9.row_add, f32[2,3,32,128]{3,2,1,0:T(8,128)S(1)} %get-tuple-element.10.col_add), custom_call_target="tpu_custom_call" | custom-call | tf_op jit(solution)/shard_map/pallas_call | solution.py:836
where the time goes:
time: 32 us; the launch traced here: 31.9 us
  Pallas kernels  31.9 us (100%)
    pallas_call x1, Pallas kernels, shards(): pl.pallas_call(kernel, out_shape=(jax.ShapeDtypeStruct((rows, COL), F32),...  30.7 us
    pallas_call x1, Pallas kernels, shards(): pl.pallas_call(closing, out_shape=jax.ShapeDtypeStruct((rows, COL), F32),...  1.17 us

commit v1 on v0

--- a/solution.py
+++ b/solution.py
@@ -180,7 +180,8 @@
                 (frac_hbm, frac_ref),
                 (base_hbm, base_ref),
                 (slots_hbm, slots_ref),
-                (x_hbm, deep.at[0, :, pl.ds(8, LON), :]),
+                (x_hbm.at[pl.ds(0, PART)], deep.at[0, pl.ds(0, PART), pl.ds(8, LON), :]),
+                (x_hbm.at[pl.ds(PART, PART)], deep.at[0, pl.ds(PART, PART), pl.ds(8, LON), :]),
             )
         )
     ]
@@ -700,12 +701,13 @@
     for part in range(2):
         if part == 0:
             message_tables()
+            copies[3].wait()
+            interpolate(0, 0)
             pl.semaphore_wait(barrier, 2 * len(AROUND) + 2 + TARGETS)
             for target in range(TARGETS):
                 idx_copy(target).start()
-            copies[3].wait()
-            interpolate(0, 0)
             send(0, 0)
+            copies[4].wait()
             interpolate(0, 1)
             send(0, 1)
             other_tables()
@@ -804,7 +806,7 @@
         vmem((2, 2, 2, FLAT, COL), F32),
         vmem((2, HALO, FLAT, COL), F32),
         vmem((2, HALO, FLAT, COL), F32),
-        dma((4,)),
+        dma((5,)),
         dma((TARGETS,)),
         dma((TARGETS,)),
         dma((2, 2, RING)),

time: 32 us -> 32 us (level)
  no operation moved by 1% of the time
where the time goes in v1:
time: 32 us; the launch traced here: 31.8 us
  Pallas kernels  31.8 us (99%)
    pallas_call x1, Pallas kernels, shards(): pl.pallas_call(kernel, out_shape=(jax.ShapeDtypeStruct((rows, COL), F32),...  30.7 us
    pallas_call x1, Pallas kernels, shards(): pl.pallas_call(closing, out_shape=jax.ShapeDtypeStruct((rows, COL), F32),...  1.17 us

profile of v1, /device:TPU:1, one launch (start us, length us, event | category | flops | bytes accessed | tf_op | source)
XLA Modules:
  0.0 31.8 jit_solution(2956543142655246993)
XLA Ops:
  0.0 30.7 %shard_map.46 = (f32[1536,128]{1,0:T(8,128)S(1)}, f32[2,3,32,128]{3,2,1,0:T(8,128)S(1)}, f32[2,3,32,128]{3,2,1,0:T(8,128)S(1)}) custom-call(f32[32,48,128]{2,1,0:T(8,128)} %bitcast.5, s32[1,240]{1,0:T(1,128)} %bitcast.8, f32[2,240]{1,0:T(2,128)} %bitcast.7, s32[1,1056]{1,0:T(1,128)} %bitcast.6), custom_call_target="tpu_custom_call" | custom-call | tf_op jit(solution)/shard_map/pallas_call | solution.py:825
  30.7 1.2 %shard_map.47 = f32[1536,128]{1,0:T(8,128)} custom-call(f32[1536,128]{1,0:T(8,128)S(1)} %get-tuple-element.8.value_ref, f32[2,3,32,128]{3,2,1,0:T(8,128)S(1)} %get-tuple-element.9.row_add, f32[2,3,32,128]{3,2,1,0:T(8,128)S(1)} %get-tuple-element.10.col_add), custom_call_target="tpu_custom_call" | custom-call | tf_op jit(solution)/shard_map/pallas_call | solution.py:838

commit v2 on v1

--- a/solution.py
+++ b/solution.py
@@ -83,23 +83,13 @@
     return result
 
 
-def shell_first(x):
-    a, b = 8.0 * (x[3] - x[0]), 45.0
-    return (
-        b * (x[1] - x[0]) - 9.0 * (x[2] - x[0]) + (x[3] - x[0]),
-        b * (x[2] - x[0]) - a,
-        b * (x[3] - x[1]) - a,
-        b * (x[3] - x[2]) - 9.0 * (x[3] - x[1]) + (x[3] - x[0]),
-    )
-
-
-def shell_second(x):
-    return (
-        2.0 * x[3] - 27.0 * x[2] + 270.0 * x[1] - 245.0 * x[0],
-        245.0 * x[0] - 490.0 * x[1] + 270.0 * x[2] - 25.0 * x[3],
-        245.0 * x[3] - 490.0 * x[2] + 270.0 * x[1] - 25.0 * x[0],
-        2.0 * x[0] - 27.0 * x[1] + 270.0 * x[2] - 245.0 * x[3],
-    )
+def shell_steps(x):
+    a, b, c = x[1] - x[0], x[2] - x[0], x[3] - x[0]
+    p, q, r = 45.0 * a, 45.0 * b, 37.0 * c
+    first = (p - 9.0 * b + c, q - 8.0 * c, r - p, r - q + 9.0 * a)
+    p, q, r = 270.0 * a, 270.0 * b, 245.0 * c
+    second = (p - 27.0 * b + 2.0 * c, q - 490.0 * a - 25.0 * c, p - 490.0 * b + r, q - 27.0 * a - r)
+    return first, second
 
 
 def turn_edges(col_add, turned):
@@ -272,7 +262,7 @@
     def interpolate(part, half):
         for pair in range(PART // 8):
             high, low = load_split(part, 2 * half + pair)
-            value = dot(jnp.concatenate([high, low, high], axis=1), mix[...])
+            value = dot(jnp.concatenate([high, low], axis=1), mix[0 : 2 * COL, :])
             value = jnp.sum(value.reshape(8, LON, SLOTS) * rows_mix[...][None], axis=1)
             blocks[part, half, 8 * pair : 8 * pair + 8, :] = value
 
@@ -289,13 +279,10 @@
             table[part, member] = blocks[part, half]
 
     def lane_pass(part):
-        def body(pair, carry):
+        for pair in range(FLAT // 8):
             high, low = load_split(part, pair)
             both = jnp.concatenate([high, low], axis=1)
-            lanes[pl.ds(pl.multiple_of(8 * LON * pair, 8), 8 * LON), :] = dot(both, band[...])
-            return carry
-
-        lax.fori_loop(0, FLAT // 8, body, 0)
+            lanes[8 * LON * pair : 8 * LON * (pair + 1), :] = dot(both, band[...])
 
     def cols_of(part):
         lane = iota((LON, COL), 1)
@@ -363,10 +350,10 @@
                 )
 
             centre = [[near(q * SHELLS + r, 0) for r in range(SHELLS)] for q in range(QUANTITIES)]
-            radial = [shell_first(x) for x in centre]
-            radial_second = [None if q == S else shell_second(centre[q]) for q in range(QUANTITIES)]
+            steps = [shell_steps(x) for x in centre]
+            radial, radial_second = [x[0] for x in steps], [x[1] for x in steps]
             emf_centre = [[near_emf(i * SHELLS + r, 0) for r in range(SHELLS)] for i in range(3)]
-            emf_radial = [None, shell_first(emf_centre[1]), shell_first(emf_centre[2])]
+            emf_radial = [None, shell_steps(emf_centre[1])[0], shell_steps(emf_centre[2])[0]]
             for r in range(SHELLS):
                 own = [centre[q][r] for q in range(QUANTITIES)]
                 g, lap = [], []
@@ -450,15 +437,13 @@
             hot = jnp.where(iota((SLOTS, COL), 0) == cell, 1.0, 0.0).astype(BF16)
             onehot[tile // 2, :, at : at + COL] = hot
 
-    def table_split(part):
-        high, low = split(table[part].reshape(GROUP * PART, SLOTS))
-        return jnp.concatenate([high, low], axis=0)
+    def rounded_table(part):
+        return table[part].reshape(GROUP * PART, SLOTS).astype(BF16)
 
     def product(both, tile):
         return dot(both, onehot[tile])
 
     def chosen(value, tile):
-        value = value[0 : GROUP * PART] + value[GROUP * PART :]
         who = jnp.broadcast_to(owner[tile, 0:1, :], (PART, SLOTS))
         total = jnp.zeros((PART, SLOTS), F32)
         for q in range(GROUP):
@@ -737,7 +722,7 @@
             prepare_picks()
         for step in range(1, GROUP):
             a_arrival(part, step).wait_recv()
-        both = table_split(part)
+        both = rounded_table(part)
         pick_all(part, both)
         main_pass(part, 0, 6)
         if part == 0:

time: 32 us -> 31.8 us (level)
  no operation moved by 1% of the time
where the time goes in v2:
time: 31.8 us; the launch traced here: 31.7 us
  Pallas kernels  31.7 us (100%)
    pallas_call x1, Pallas kernels, shards(): pl.pallas_call(kernel, out_shape=(jax.ShapeDtypeStruct((rows, COL), F32),...  30.5 us
    pallas_call x1, Pallas kernels, shards(): pl.pallas_call(closing, out_shape=jax.ShapeDtypeStruct((rows, COL), F32),...  1.17 us

profile of v2, /device:TPU:1, one launch (start us, length us, event | category | flops | bytes accessed | tf_op | source)
XLA Modules:
  0.0 31.7 jit_solution(13044104808813151067)
XLA Ops:
  0.0 30.5 %shard_map.46 = (f32[1536,128]{1,0:T(8,128)S(1)}, f32[2,3,32,128]{3,2,1,0:T(8,128)S(1)}, f32[2,3,32,128]{3,2,1,0:T(8,128)S(1)}) custom-call(f32[32,48,128]{2,1,0:T(8,128)} %bitcast.5, s32[1,240]{1,0:T(1,128)} %bitcast.8, f32[2,240]{1,0:T(2,128)} %bitcast.7, s32[1,1056]{1,0:T(1,128)} %bitcast.6), custom_call_target="tpu_custom_call" | custom-call | tf_op jit(solution)/shard_map/pallas_call | solution.py:810
  30.5 1.2 %shard_map.47 = f32[1536,128]{1,0:T(8,128)} custom-call(f32[1536,128]{1,0:T(8,128)S(1)} %get-tuple-element.8.value_ref, f32[2,3,32,128]{3,2,1,0:T(8,128)S(1)} %get-tuple-element.9.row_add, f32[2,3,32,128]{3,2,1,0:T(8,128)S(1)} %get-tuple-element.10.col_add), custom_call_target="tpu_custom_call" | custom-call | tf_op jit(solution)/shard_map/pallas_call | solution.py:823

commit v3 on v2

--- a/solution.py
+++ b/solution.py
@@ -112,17 +112,17 @@
     copies = []
     for half in range(2):
         edge = jnp.transpose(turned[half])[0:LON, :]
-        for chunk in range(2):
-            first = half * (FLAT // 2) + 8 * chunk
-            for q in range(8):
+        for chunk in range(4):
+            first = half * (FLAT // 2) + 4 * chunk
+            for q in range(4):
                 at = (first + q) * LON
-                ready[at : at + LON, :] = value_ref[at : at + LON, :] + field_edge(edge, 8 * chunk + q)
+                ready[at : at + LON, :] = value_ref[at : at + LON, :] + field_edge(edge, 4 * chunk + q)
             for side in range(2):
                 for j in range(HALO):
-                    rows = pl.ds(first * LON + (j if side == 0 else LON - HALO + j), 8, stride=LON)
-                    ready[rows, :] = ready[rows, :] + row_add[side, j, first : first + 8, :]
-            rows = pl.ds(first * LON, 8 * LON)
-            copy = pltpu.make_async_copy(ready.at[rows, :], out_hbm.at[rows, :], sem.at[2 * half + chunk])
+                    rows = pl.ds(first * LON + (j if side == 0 else LON - HALO + j), 4, stride=LON)
+                    ready[rows, :] = ready[rows, :] + row_add[side, j, first : first + 4, :]
+            rows = pl.ds(first * LON, 4 * LON)
+            copy = pltpu.make_async_copy(ready.at[rows, :], out_hbm.at[rows, :], sem.at[4 * half + chunk])
             copy.start()
             copies.append(copy)
     for copy in copies:
@@ -262,7 +262,7 @@
     def interpolate(part, half):
         for pair in range(PART // 8):
             high, low = load_split(part, 2 * half + pair)
-            value = dot(jnp.concatenate([high, low], axis=1), mix[0 : 2 * COL, :])
+            value = dot(jnp.concatenate([high, low, high], axis=1), mix[...])
             value = jnp.sum(value.reshape(8, LON, SLOTS) * rows_mix[...][None], axis=1)
             blocks[part, half, 8 * pair : 8 * pair + 8, :] = value
 
@@ -437,13 +437,15 @@
             hot = jnp.where(iota((SLOTS, COL), 0) == cell, 1.0, 0.0).astype(BF16)
             onehot[tile // 2, :, at : at + COL] = hot
 
-    def rounded_table(part):
-        return table[part].reshape(GROUP * PART, SLOTS).astype(BF16)
+    def table_split(part):
+        high, low = split(table[part].reshape(GROUP * PART, SLOTS))
+        return jnp.concatenate([high, low], axis=0)
 
     def product(both, tile):
         return dot(both, onehot[tile])
 
     def chosen(value, tile):
+        value = value[0 : GROUP * PART] + value[GROUP * PART :]
         who = jnp.broadcast_to(owner[tile, 0:1, :], (PART, SLOTS))
         total = jnp.zeros((PART, SLOTS), F32)
         for q in range(GROUP):
@@ -688,13 +690,13 @@
             message_tables()
             copies[3].wait()
             interpolate(0, 0)
+            copies[4].wait()
+            interpolate(0, 1)
             pl.semaphore_wait(barrier, 2 * len(AROUND) + 2 + TARGETS)
+            send(0, 0)
+            send(0, 1)
             for target in range(TARGETS):
                 idx_copy(target).start()
-            send(0, 0)
-            copies[4].wait()
-            interpolate(0, 1)
-            send(0, 1)
             other_tables()
         else:
             send(1, 0)
@@ -722,7 +724,7 @@
             prepare_picks()
         for step in range(1, GROUP):
             a_arrival(part, step).wait_recv()
-        both = rounded_table(part)
+        both = table_split(part)
         pick_all(part, both)
         main_pass(part, 0, 6)
         if part == 0:
@@ -825,7 +827,7 @@
         out_shape=jax.ShapeDtypeStruct((rows, COL), F32),
         in_specs=[pl.BlockSpec(memory_space=pltpu.VMEM)] * 3,
         out_specs=pl.BlockSpec(memory_space=pltpu.HBM),
-        scratch_shapes=[vmem((2, COL, COL), F32), vmem((rows, COL), F32), dma((4,))],
+        scratch_shapes=[vmem((2, COL, COL), F32), vmem((rows, COL), F32), dma((8,))],
         compiler_params=pltpu.CompilerParams(vmem_limit_bytes=16 * 1024 * 1024),
     )(value, row_add, col_add)
     return result.reshape(state.shape)

time: 31.8 us -> 32.1 us (level)
  no operation moved by 1% of the time
where the time goes in v3:
time: 32.1 us; the launch traced here: 32 us
  Pallas kernels  32 us (100%)
    pallas_call x1, Pallas kernels, shards(): pl.pallas_call(kernel, out_shape=(jax.ShapeDtypeStruct((rows, COL), F32),...  30.8 us
    pallas_call x1, Pallas kernels, shards(): pl.pallas_call(closing, out_shape=jax.ShapeDtypeStruct((rows, COL), F32),...  1.17 us

profile of v3, /device:TPU:1, one launch (start us, length us, event | category | flops | bytes accessed | tf_op | source)
XLA Modules:
  0.0 32.0 jit_solution(8367553866273510357)
XLA Ops:
  0.0 30.8 %shard_map.46 = (f32[1536,128]{1,0:T(8,128)S(1)}, f32[2,3,32,128]{3,2,1,0:T(8,128)S(1)}, f32[2,3,32,128]{3,2,1,0:T(8,128)S(1)}) custom-call(f32[32,48,128]{2,1,0:T(8,128)} %bitcast.5, s32[1,240]{1,0:T(1,128)} %bitcast.8, f32[2,240]{1,0:T(2,128)} %bitcast.7, s32[1,1056]{1,0:T(1,128)} %bitcast.6), custom_call_target="tpu_custom_call" | custom-call | tf_op jit(solution)/shard_map/pallas_call | solution.py:812
  30.8 1.2 %shard_map.47 = f32[1536,128]{1,0:T(8,128)} custom-call(f32[1536,128]{1,0:T(8,128)S(1)} %get-tuple-element.8.value_ref, f32[2,3,32,128]{3,2,1,0:T(8,128)S(1)} %get-tuple-element.9.row_add, f32[2,3,32,128]{3,2,1,0:T(8,128)S(1)} %get-tuple-element.10.col_add), custom_call_target="tpu_custom_call" | custom-call | tf_op jit(solution)/shard_map/pallas_call | solution.py:825

commit v4 on v3

--- a/solution.py
+++ b/solution.py
@@ -25,7 +25,7 @@
 SPARE = SIDE - COL
 PART = FLAT // 2
 TARGETS = 2 * GROUPS
-TILES = 12
+TILES = 8
 RING = 4
 FOLD = PART // 8
 STRIDE = LON + 16
@@ -132,9 +132,9 @@
 def kernel(
     x_hbm, base_hbm, frac_hbm, slots_hbm, out_ref, row_add, col_add,
     deep, base_ref, frac_ref, slots_ref, emf, lanes, mix, cols_mix, rows_mix, rows_split, band, onehot, owner, turned,
-    blocks, table, idx_out, idx_in, rest_rows, picked, picked_rows, got_cols, got_rows, row_out, row_in, col_own, col_out, col_in,
+    blocks, table, idx_out, idx_in, idx_ends, rest_rows, picked, picked_rows, got_cols, got_rows, row_out, row_in, col_own, col_out, col_in,
     row_halo, col_halo,
-    in_sem, idx_send, idx_recv, a_send, a_recv, s_send, b_send, b_recv, l_send, l_recv, r_send, r_recv, c_send, c_recv,
+    in_sem, idx_send, idx_recv, e_send, e_recv, a_send, a_recv, s_send, b_send, b_recv, l_send, l_recv, r_send, r_recv, c_send, c_recv,
 ):
     panel, lon, col = lax.axis_index("panel"), lax.axis_index("lon"), lax.axis_index("colat")
     n_lon, n_col = lax.axis_size("lon"), lax.axis_size("colat")
@@ -150,12 +150,24 @@
 
     sibling = (panel, lon + 1 - 2 * core, col)
     origin = core * GROUPS + mine
+    lon_edge = jnp.logical_or(lon == 0, lon == n_lon - 1)
+    target_col, target_core = (col >> 1) * (n_col - 1), (col ^ (col >> 1)) & 1
+    source_col = col ^ core
 
     def row_device(step, half):
         return (panel, 2 * mine + half, (col + step) & (n_col - 1))
 
-    def target_device(target):
-        return (other, 2 * (target & (GROUPS - 1)) + (target >> 3), col)
+    def side_device(target):
+        return (other, 2 * target + target_core, target_col)
+
+    def end_device(side):
+        return (other, side * (n_lon - 1), col)
+
+    def side_source(source):
+        return (other, 2 * (source % GROUPS) + source // GROUPS, source_col)
+
+    def end_source(source):
+        return (other, 2 * (source % GROUPS) + source // GROUPS, col)
 
     def remote(src, dst, send, recv, device):
         return pltpu.make_async_remote_copy(
@@ -183,8 +195,21 @@
         for half in range(2):
             pl.semaphore_signal(barrier, inc=1, device_id=row_device(step, half), device_id_type=MESH)
     pl.semaphore_signal(barrier, inc=1, device_id=sibling, device_id_type=MESH)
-    for target in range(TARGETS):
-        pl.semaphore_signal(barrier, inc=1, device_id=target_device(target), device_id_type=MESH)
+    for target in range(GROUPS):
+        pl.semaphore_signal(barrier, inc=1, device_id=side_device(target), device_id_type=MESH)
+    for side in range(2):
+        pl.semaphore_signal(barrier, inc=1, device_id=end_device(side), device_id_type=MESH)
+
+    @pl.when(col_edge)
+    def _():
+        for source in range(TARGETS):
+            pl.semaphore_signal(barrier, inc=1, device_id=side_source(source), device_id_type=MESH)
+
+    @pl.when(lon_edge)
+    def _():
+        for source in range(TARGETS):
+            pl.semaphore_signal(barrier, inc=1, device_id=end_source(source), device_id_type=MESH)
+
     pl.semaphore_signal(barrier, inc=1, device_id=(panel, outer, col), device_id_type=MESH)
 
     copies[0].wait()
@@ -416,16 +441,17 @@
 
     def prepare_picks():
         for tile in range(2 * TILES):
-            if tile < TARGETS:
+            if tile < GROUPS:
                 slot = idx_in[tile, 0:1, :]
-            elif tile < TARGETS + 2:
-                first = (tile - TARGETS) * GROUPS
-                slot = idx_in[first, 1:2, :]
+            elif tile == GROUPS:
+                slot = idx_in[0, 1:2, :]
                 for q in range(1, GROUPS):
-                    slot = jnp.maximum(slot, pltpu.roll(idx_in[first + q], SPARE * q, 1)[1:2, :])
+                    slot = jnp.maximum(slot, pltpu.roll(idx_in[q], SPARE * q, 1)[1:2, :])
+            elif tile <= GROUPS + 2 * HALO:
+                side, h = divmod(tile - GROUPS - 1, HALO)
+                slot = idx_ends[side, 2 + h : 3 + h, :]
             else:
-                side, h = divmod(tile - TARGETS - 2, HALO)
-                slot = idx_in[side * (TARGETS - 1), 2 + h : 3 + h, :]
+                slot = jnp.full((1, COL), -1, I32)
             slot = slot - mine * (GROUP * OUT)
             who = jnp.zeros_like(slot)
             for q in range(1, GROUP):
@@ -452,48 +478,39 @@
             total = jnp.where(who == q, value[q * PART : (q + 1) * PART, :], total)
         return total[:, 0:COL], total[:, COL : 2 * COL]
 
-    def fold(rests):
+    def fold(rest):
         turn = (lax.div(iota((8, COL), 1), SPARE) - iota((8, COL), 0)) & 7
-        for half, rest in enumerate(rests):
-            for s in range(FOLD):
-                total = jnp.zeros((8, COL), F32)
-                for d in range(8):
-                    moved = rest[8 * s : 8 * s + 8, :]
-                    if d:
-                        moved = pltpu.roll(pltpu.roll(moved, SPARE * d, 1), 8 - d, 0)
-                    total = jnp.where(turn == d, moved, total)
-                rest_rows[half, s] = total
+        for s in range(FOLD):
+            total = jnp.zeros((8, COL), F32)
+            for d in range(8):
+                moved = rest[8 * s : 8 * s + 8, :]
+                if d:
+                    moved = pltpu.roll(pltpu.roll(moved, SPARE * d, 1), 8 - d, 0)
+                total = jnp.where(turn == d, moved, total)
+            rest_rows[s] = total
 
     def pick_all(part, both):
-        sides = [(step + mine) & (TARGETS // 2 - 1) for step in range(TARGETS // 2)]
-        extra = list(range(TARGETS // 2 + 1, TILES))
-        ends, value = [], product(both, extra[0])
-        for tile, after in zip(extra, extra[1:] + [None]):
+        order = list(range(GROUPS // 2, TILES)) + [(step + mine) & (GROUPS // 2 - 1) for step in range(GROUPS // 2)]
+        ends, value = [], product(both, order[0])
+        for place, tile in enumerate(order):
             now = value
-            if after is not None:
-                value = product(both, after)
-            ends += chosen(now, tile)
-        for side in range(2):
-            for h in range(HALO):
-                picked_rows[part, side, h] = ends[side * HALO + h]
-        for side in range(2):
-            l_copy(part, side).start()
-
-        @pl.when(col_edge)
-        def _():
-            now, value = product(both, TARGETS // 2), product(both, sides[0])
-            fold(chosen(now, TARGETS // 2))
-            for step, tile in enumerate(sides):
-                now = value
-                if step + 1 < len(sides):
-                    value = product(both, sides[step + 1])
-                for i, end in enumerate(chosen(now, tile)):
+            if place + 1 < len(order):
+                value = product(both, order[place + 1])
+            pair = chosen(now, tile)
+            if place < TILES - GROUPS // 2:
+                ends += pair
+                if place == TILES - GROUPS // 2 - 1:
+                    for side in range(2):
+                        for h in range(HALO):
+                            picked_rows[part, side, h] = ends[1 + side * HALO + h]
+                        l_copy(part, side).start()
+                    fold(ends[0])
+            else:
+                for i, end in enumerate(pair):
                     target = 2 * tile + i
                     picked[part, target, 0:PART, :] = end
                     for s in range(FOLD):
-                        picked[part, target, PART + s : PART + s + 1, :] = rest_rows[
-                            tile >> 2, s, pl.ds(target & (GROUPS - 1), 1), :
-                        ]
+                        picked[part, target, PART + s : PART + s + 1, :] = rest_rows[s, pl.ds(target, 1), :]
                 for i in range(2):
                     b_copy(part, 2 * tile + i).start()
 
@@ -581,7 +598,7 @@
     def b_copy(part, target):
         return remote(
             picked.at[part, target], got_cols.at[part, origin], b_send.at[part, target], b_recv.at[part, origin],
-            target_device(target),
+            side_device(target),
         )
 
     def b_arrival(part, source):
@@ -593,7 +610,7 @@
     def l_copy(part, side):
         return remote(
             picked_rows.at[part, side], got_rows.at[part, origin], l_send.at[part, side], l_recv.at[part, origin],
-            target_device(side * (TARGETS - 1)),
+            end_device(side),
         )
 
     def l_arrival(part, source):
@@ -614,13 +631,17 @@
             (panel, lon, col_up if side == 0 else col_down),
         )
 
-    def idx_copy(target):
-        return remote(
-            idx_out, idx_in.at[origin], idx_send.at[target], idx_recv.at[origin], target_device(target)
-        )
-
-    def idx_arrival(source):
-        return remote(idx_out, idx_in.at[source], idx_send.at[0], idx_recv.at[source], (other, lon, col))
+    def idx_copy(source):
+        return remote(idx_out, idx_in.at[mine], idx_send.at[source], idx_recv.at[mine], side_source(source))
+
+    def idx_arrival(target):
+        return remote(idx_out, idx_in.at[target], idx_send.at[0], idx_recv.at[target], (other, lon, col))
+
+    def end_copy(source):
+        return remote(idx_out, idx_ends.at[core], e_send.at[source], e_recv.at[core], end_source(source))
+
+    def end_arrival(side):
+        return remote(idx_out, idx_ends.at[side], e_send.at[0], e_recv.at[side], (other, lon, col))
 
     def inner_sides(part):
         for side in range(2):
@@ -692,11 +713,22 @@
             interpolate(0, 0)
             copies[4].wait()
             interpolate(0, 1)
-            pl.semaphore_wait(barrier, 2 * len(AROUND) + 2 + TARGETS)
+            greetings = 2 * len(AROUND) + 2 + GROUPS + 2
+            greetings = greetings + jnp.where(col_edge, TARGETS, 0) + jnp.where(lon_edge, TARGETS, 0)
+            pl.semaphore_wait(barrier, greetings)
             send(0, 0)
             send(0, 1)
-            for target in range(TARGETS):
-                idx_copy(target).start()
+
+            @pl.when(col_edge)
+            def _():
+                for source in range(TARGETS):
+                    idx_copy(source).start()
+
+            @pl.when(lon_edge)
+            def _():
+                for source in range(TARGETS):
+                    end_copy(source).start()
+
             other_tables()
         else:
             send(1, 0)
@@ -719,8 +751,10 @@
         lane_pass(part)
         emf_pass(part)
         if part == 0:
-            for source in range(TARGETS):
-                idx_arrival(source).wait_recv()
+            for target in range(GROUPS):
+                idx_arrival(target).wait_recv()
+            for side in range(2):
+                end_arrival(side).wait_recv()
             prepare_picks()
         for step in range(1, GROUP):
             a_arrival(part, step).wait_recv()
@@ -733,8 +767,16 @@
         inner_sides(part)
         outer_sides(part)
 
-    for target in range(TARGETS):
-        idx_copy(target).wait_send()
+    @pl.when(col_edge)
+    def _():
+        for source in range(TARGETS):
+            idx_copy(source).wait_send()
+
+    @pl.when(lon_edge)
+    def _():
+        for source in range(TARGETS):
+            end_copy(source).wait_send()
+
     for part in range(2):
         for half in range(2):
             for step in AROUND:
@@ -751,11 +793,8 @@
             def _():
                 col_copy(part, side).wait_send()
 
-
-        @pl.when(col_edge)
-        def _():
-            for target in range(TARGETS):
-                b_copy(part, target).wait_send()
+        for target in range(GROUPS):
+            b_copy(part, target).wait_send()
 
 
 def shards(state, send_base, send_frac, recv_slots):
@@ -780,9 +819,10 @@
         vmem((2, 2, PART, SLOTS), F32),
         vmem((2, GROUP, PART, SLOTS), F32),
         vmem((8, COL), I32),
-        vmem((TARGETS, 8, COL), I32),
-        vmem((2, FOLD, 8, COL), F32),
-        vmem((2, TARGETS, PART + FOLD, COL), F32),
+        vmem((GROUPS, 8, COL), I32),
+        vmem((2, 8, COL), I32),
+        vmem((FOLD, 8, COL), F32),
+        vmem((2, GROUPS, PART + FOLD, COL), F32),
         vmem((2, 2, HALO, PART, COL), F32),
         vmem((2, TARGETS, PART + FOLD, COL), F32),
         vmem((2, TARGETS, HALO, PART, COL), F32),
@@ -795,11 +835,13 @@
         vmem((2, HALO, FLAT, COL), F32),
         dma((5,)),
         dma((TARGETS,)),
+        dma((GROUPS,)),
         dma((TARGETS,)),
+        dma((2,)),
         dma((2, 2, RING)),
         dma((2, GROUP)),
         dma((2,)),
-        dma((2, TARGETS)),
+        dma((2, GROUPS)),
         dma((2, TARGETS)),
         dma((2, 2)),
         dma((2, TARGETS)),

time: 32.1 us -> 32.7 us (1.019)
  Pallas kernels: 32 us -> 32.6 us
    pallas_call x1, Pallas kernels: 30.8 us -> 31.4 us  [shards(): pl.pallas_call(kernel, out_shape=(jax.ShapeDtypeStruct((rows, COL), F32),...]
where the time goes in v4:
time: 32.7 us; the launch traced here: 32.6 us
  Pallas kernels  32.6 us (100%)
    pallas_call x1, Pallas kernels, shards(): pl.pallas_call(kernel, out_shape=(jax.ShapeDtypeStruct((rows, COL), F32),...  31.4 us
    pallas_call x1, Pallas kernels, shards(): pl.pallas_call(closing, out_shape=jax.ShapeDtypeStruct((rows, COL), F32),...  1.17 us

profile of v4, /device:TPU:1, one launch (start us, length us, event | category | flops | bytes accessed | tf_op | source)
XLA Modules:
  0.0 32.6 jit_solution(14874243359845119281)
XLA Ops:
  0.0 31.4 %shard_map.46 = (f32[1536,128]{1,0:T(8,128)S(1)}, f32[2,3,32,128]{3,2,1,0:T(8,128)S(1)}, f32[2,3,32,128]{3,2,1,0:T(8,128)S(1)}) custom-call(f32[32,48,128]{2,1,0:T(8,128)} %bitcast.5, s32[1,240]{1,0:T(1,128)} %bitcast.8, f32[2,240]{1,0:T(2,128)} %bitcast.7, s32[1,1056]{1,0:T(1,128)} %bitcast.6), custom_call_target="tpu_custom_call" | custom-call | tf_op jit(solution)/shard_map/pallas_call | solution.py:854
  31.4 1.2 %shard_map.47 = f32[1536,128]{1,0:T(8,128)} custom-call(f32[1536,128]{1,0:T(8,128)S(1)} %get-tuple-element.8.value_ref, f32[2,3,32,128]{3,2,1,0:T(8,128)S(1)} %get-tuple-element.9.row_add, f32[2,3,32,128]{3,2,1,0:T(8,128)S(1)} %get-tuple-element.10.col_add), custom_call_target="tpu_custom_call" | custom-call | tf_op jit(solution)/shard_map/pallas_call | solution.py:867
